TPU v7x, 1024 devices: a whole 4x4x32 slice. The times are simulated.
1024 devices in a mesh: row: 128 (over z, x), col: 4 (over y), rep: 2 (over core).
Axes of the slice: x: 4, y: 4, z: 32, core: 2. Of those that a mesh axis runs over, the one named last changes fastest.
Arguments:
- output_grad: bfloat16 [131072, 256], P(('row', 'col', 'rep')), may hold values from -6 to 6
- pooled: bfloat16 [131072, 64], P(('row', 'col', 'rep')), may hold values from -6 to 6
- bag_owners: int32 [131072, 4], P(('row', 'col', 'rep')), may hold values from 0 to 127, all different within a row; in each aligned block of 128 rows (0 to 127, 128 to 255, ...) at most 6 rows name the same one
- bag_rows: int32 [131072, 4], P(('row', 'col', 'rep')), may hold values from 0 to 4095
- bag_weights: float32 [131072, 4], P(('row', 'col', 'rep')), may hold values from 0.5 to 2
- embed_table: float32 [524288, 64], P('row'), may hold values from -6 to 6
- table_state: float32 [524288], P('row'), may hold values from 0.5 to 8
- projection: float32 [64, 256], replicated, may hold values from -0.75 to 0.75
- projection_state: float32 [64, 256], replicated, may hold values from 32768 to 2097152
Outputs:
- new_table: float32 [524288, 64], P('row')
- new_table_state: float32 [524288], P('row')
- new_projection: float32 [64, 256], replicated
- new_projection_state: float32 [64, 256], replicated
Inputs may be any that keep to these rules, and one draw needn't show every extreme that they name: `bag_owners`: the 4 entries of a sample name different owners; among the 128 samples of one device no owner is named by more than 6 entries, a bound that some block reaches.
All inputs are finite; a program needn't handle non-finite values.
Results may differ from a plain program's by a relative error of at most 0.0013.
Values may be sent and summed in bfloat16 or wider, within the bound.
No kernel may reach another device: no remote copies, remote signals or barrier semaphores. Data moves between devices by JAX's collectives and lax.ppermute only.
A program may use at most 32 MiB of HBM per device.

v0:
```python
import jax
import jax.numpy as jnp
from jax import lax
from jax.sharding import PartitionSpec as P

learn_rate = 0.5
epsilon = 1e-06


def scatter_rows(got_rows, got_ids, table_rows, row_width):
    flat_rows = got_rows.reshape(-1, row_width).astype(jnp.float32)
    empty = jnp.zeros((table_rows, row_width), jnp.float32)
    return empty.at[got_ids.reshape(-1)].add(flat_rows, mode="drop")


def shards(
    output_grad,
    pooled,
    bag_owners,
    bag_rows,
    bag_weights,
    embed_table,
    table_state,
    projection,
    projection_state,
):
    owner_count = lax.axis_size("row")
    samples, bag_size = bag_owners.shape
    table_rows, row_width = embed_table.shape
    slot_count = max(2, (3 * samples * bag_size // 2 + owner_count - 1) // owner_count)
    projection_low = projection.astype(jnp.bfloat16)
    pool_grad = jnp.dot(output_grad, projection_low.T, preferred_element_type=jnp.float32)
    grad_rows = (bag_weights[:, :, None] * pool_grad[:, None, :]).astype(jnp.bfloat16)
    grad_rows = grad_rows.reshape(samples * bag_size, row_width)
    owner_flat = bag_owners.reshape(-1)
    owner_hits = (owner_flat[:, None] == jnp.arange(owner_count, dtype=jnp.int32)[None, :]).astype(
        jnp.int32
    )
    earlier = jnp.cumsum(owner_hits, axis=0) - owner_hits
    slot_rank = jnp.sum(earlier * owner_hits, axis=1)
    slot_index = owner_flat * slot_count + slot_rank
    send_rows = (
        jnp.zeros((owner_count * slot_count, row_width), jnp.bfloat16).at[slot_index].set(grad_rows)
    )
    send_rows = send_rows.reshape(owner_count, slot_count * row_width)
    send_ids = (
        jnp.full((owner_count * slot_count,), table_rows, jnp.int32)
        .at[slot_index]
        .set(bag_rows.reshape(-1))
    )
    send_ids = send_ids.reshape(owner_count, slot_count)
    got_rows, got_ids = (
        lax.all_to_all(send_rows, "row", split_axis=0, concat_axis=0, tiled=True),
        lax.all_to_all(send_ids, "row", split_axis=0, concat_axis=0, tiled=True),
    )
    local_grad = scatter_rows(got_rows, got_ids, table_rows, row_width)
    dense_grad = lax.psum(local_grad, ("col", "rep"))
    new_table_state = table_state + jnp.mean(dense_grad * dense_grad, axis=1)
    new_table = embed_table - learn_rate * dense_grad / (
        jnp.sqrt(new_table_state)[:, None] + epsilon
    )
    weight_grad = lax.dot_general(
        pooled, output_grad, (((0,), (0,)), ((), ())), preferred_element_type=jnp.float32
    )
    total_grad = lax.psum(weight_grad, ("row", "col", "rep"))
    new_projection_state = projection_state + total_grad * total_grad
    new_projection = projection - learn_rate * total_grad / (
        jnp.sqrt(new_projection_state) + epsilon
    )
    return (new_table, new_table_state, new_projection, new_projection_state)


def solution(mesh):
    placed = (
        P(("row", "col", "rep"), None),
        P(("row", "col", "rep"), None),
        P(("row", "col", "rep"), None),
        P(("row", "col", "rep"), None),
        P(("row", "col", "rep"), None),
        P("row", None),
        P("row"),
        P(),
        P(),
    )
    return jax.shard_map(
        shards,
        mesh=mesh,
        in_specs=placed,
        out_specs=(P("row", None), P("row"), P(), P()),
        check_vma=False,
    )
```

profile of v0, /device:TPU:1, one launch (start us, length us, event | category | flops | bytes accessed | tf_op | source)
XLA Modules:
  0.0 1031.7 jit_solution(612160926806521046)
XLA Ops:
  7.2 0.8 copy.25
  8.3 0.7 broadcast_multiply_fusion
  9.6 0.8 copy.29
  10.8 2.4 scatter_custom_fusion
  13.2 0.8 all_to_all.12
  14.0 33.6 %all-to-all-start = ((s32[128,1,6]{2,1,0:T(1,128)}), s32[128,1,6]{2,1,0:T(1,128)S(1)}, u32[]{:S(2)}, u32[]{:S(2)}) async-start(s32[128,1,6]{2,1,0:T(1,128)} %bitcast.5), calls=%async_computation | async-start | bytes 131072 | tf_op jit(solution)/shard_map/all_to_all | solution.py:54
  48.0 1.9 scatter_custom_fusion.1
  50.6 1.2 reduce.8
  51.8 0.8 reshape.154
  52.6 18.1 %all-to-all-done = s32[128,1,6]{2,1,0:T(1,128)S(1)} async-done(((s32[128,1,6]{2,1,0:T(1,128)}), s32[128,1,6]{2,1,0:T(1,128)S(1)}, u32[]{:S(2)}, u32[]{:S(2)}) %all-to-all-start) | async-done | bytes 3104 | tf_op jit(solution)/shard_map/all_to_all | solution.py:54
  70.7 8.2 all-to-all-start.1
  78.9 0.8 fusion.15
  80.5 0.8 reduce.7
  81.5 22.5 %all-to-all-done.1 = bf16[128,2,192]{2,1,0:T(2,128)(2,1)S(1)} async-done(((bf16[128,2,192]{2,1,0:T(2,128)(2,1)}), bf16[128,2,192]{2,1,0:T(2,128)(2,1)S(1)}, u32[]{:S(2)}, u32[]{:S(2)}) %all-to-all-start.1) | async-done | bytes 98336 | tf_op jit(solution)/shard_map/all_to_all | solution.py:53
  104.1 0.5 convert_reduce_fusion
  104.8 7.4 scatter_custom_fusion.2
  112.3 0.6 copy.34
  112.9 818.5 %all-reduce.5.cloned.1.call-done = f32[64,256]{1,0:T(8,128)} async-done(((f32[64,256]{1,0:T(8,128)}), f32[64,256]{1,0:T(8,128)}) %all-reduce.5.cloned.1.call-update) | async-done | bytes 65552 | tf_op jit(solution)/shard_map/psum | solution.py:65
  931.4 1.5 divide_subtract_fusion.1
  932.9 84.2 %all-reduce.3.cloned.1.call-done = f32[4096,64]{1,0:T(8,128)} async-done(((f32[4096,64]{1,0:T(8,128)}), f32[4096,64]{1,0:T(8,128)}) %all-reduce.3.cloned.1.call-update) | async-done | bytes 1048592 | tf_op jit(solution)/shard_map/psum | solution.py:57
  1017.0 2.3 multiply_reduce_fusion
  1019.4 0.6 sqrt_add_fusion
  1020.0 1.7 divide_subtract_fusion
  1021.7 3.1 copy.35
  (46 shorter events, 3.5 us)
Async XLA Ops:
  7.2 40.4 %copy-start = (bf16[128,256]{1,0:T(8,128)(2,1)S(1)}, bf16[128,256]{1,0:T(8,128)(2,1)}, u32[]{:S(2)}) copy-start(bf16[128,256]{1,0:T(8,128)(2,1)} %param.9) | copy-start | bytes 196612
  7.2 40.4 %copy-start.3 = (f32[64,256]{1,0:T(8,128)S(1)}, f32[64,256]{1,0:T(8,128)}, u32[]{:S(2)}) copy-start(f32[64,256]{1,0:T(8,128)} %param.16) | copy-start | bytes 196612
  7.2 40.5 %copy-start.7 = (f32[128,4]{0,1:T(4,128)S(1)}, f32[128,4]{0,1:T(4,128)}, u32[]{:S(2)}) copy-start(f32[128,4]{0,1:T(4,128)} %param.13) | copy-start | bytes 6148
  9.3 69.7 %copy-start.5 = (bf16[128,64]{0,1:T(8,128)(2,1)S(1)}, bf16[128,64]{0,1:T(8,128)(2,1)}, u32[]{:S(2)}) copy-start(bf16[128,64]{0,1:T(8,128)(2,1)} %param.10) | copy-start | bytes 49156
  14.0 56.7 %all-to-all-start = ((s32[128,1,6]{2,1,0:T(1,128)}), s32[128,1,6]{2,1,0:T(1,128)S(1)}, u32[]{:S(2)}, u32[]{:S(2)}) async-start(s32[128,1,6]{2,1,0:T(1,128)} %bitcast.5), calls=%async_computation | async-start | bytes 131072 | tf_op jit(solution)/shard_map/all_to_all | solution.py:54
  70.7 33.3 %all-to-all-start.1 = ((bf16[128,2,192]{2,1,0:T(2,128)(2,1)}), bf16[128,2,192]{2,1,0:T(2,128)(2,1)S(1)}, u32[]{:S(2)}, u32[]{:S(2)}) async-start(bf16[128,2,192]{2,1,0:T(2,128)(2,1)} %reshape.154), calls=%async_computation.1 | async-start | bytes 262144 | tf_op jit(solution)/shard_map/all_to_all | solution.py:53
  78.9 852.5 %all-reduce.5.cloned.1.call-start = ((), (), s32[]{:S(2)}) async-start(), calls=%async_computation.3 | async-start | bytes 131072 | tf_op jit(solution)/shard_map/psum | solution.py:65
  79.7 937.3 %all-reduce.3.cloned.1.call-start = ((), (), s32[]{:S(2)}) async-start(), calls=%async_computation.2 | async-start | bytes 4194304 | tf_op jit(solution)/shard_map/psum | solution.py:57
  104.8 7.4 copy-start.2
  112.2 819.1 %copy-start.4 = (f32[64,256]{1,0:T(8,128)S(1)}, f32[64,256]{1,0:T(8,128)}, u32[]{:S(2)}) copy-start(f32[64,256]{1,0:T(8,128)} %param.17) | copy-start | bytes 196612
  112.3 907.1 %copy-start.6 = (f32[4096]{0:T(1024)S(1)}, f32[4096]{0:T(1024)}, u32[]{:S(2)}) copy-start(f32[4096]{0:T(1024)} %param.15) | copy-start | bytes 49156
  1017.0 3.0 copy-start.1
Sparse Core Ops, SparseCore 0:
  85.7 845.5 all-reduce.4
  933.8 83.1 all-reduce.2
where the time goes:
time: 1030 us
  waiting for transfers between devices  943 us (92%)
  starting transfers between devices  42.1 us (4%)
  other arithmetic  19.3 us (2%)
  between operations  14.3 us (1%)
  local copies, waits for them, and re-layouts  12 us (1%)
    psum x1, waiting for transfers between devices, shards(): total_grad = lax.psum(weight_grad, ('row', 'col', 'rep'))  818 us
    psum x1, waiting for transfers between devices, shards(): dense_grad = lax.psum(local_grad, ('col', 'rep'))  84.2 us
    all_to_all x1, starting transfers between devices, shards(): lax.all_to_all(send_ids, 'row', split_axis=0, concat_axis=0, tiled=True)  33.6 us
    all_to_all x1, waiting for transfers between devices, shards(): lax.all_to_all(send_rows, 'row', split_axis=0, concat_axis=0, tiled=True)  22.5 us
  transfers between devices with their start and end apart: 4, of which 4 were waited for; matrix products, arithmetic and copies ran while one was open for 2% of the time, Pallas kernels for 0%

commit v1 on v0

v1 whole, which is shorter than its diff:
```python
import functools

import jax
import jax.numpy as jnp
from jax import lax
from jax.experimental import pallas as pl
from jax.experimental.pallas import tpu as pltpu
from jax.sharding import Mesh
from jax.sharding import PartitionSpec as P

learn_rate = 0.5
epsilon = 1e-06

X = 4
CAP = 6
QUAD = 4
PLANE = ("x", "col", "rep")
LOW = jnp.bfloat16
FULL = jnp.float32

NT = (((1,), (1,)), ((), ()))
TN = (((0,), (0,)), ((), ()))


def dot(a, b, dims):
    return lax.dot_general(a, b, dims, preferred_element_type=FULL)


def iota(shape, dim):
    return lax.broadcasted_iota(jnp.int32, shape, dim)


def halves(value):
    high = value.astype(LOW).astype(FULL)
    return jnp.concatenate([high, value - high], axis=0)


def route_kernel(*refs):
    ins, outs, held, sems = refs[:6], refs[6:8], refs[8:14], refs[14]
    copies = [
        pltpu.make_async_copy(ins[n], held[n], sems.at[n]) for n in range(len(ins))
    ]
    for copy in copies:
        copy.start()
    for copy in copies:
        copy.wait()
    output_grad, pooled_t, projection, owners, rows, weights = held
    shares, out = outs

    grad = jnp.dot(pooled_t[...], output_grad[...], preferred_element_type=FULL)
    for i in range(shares.shape[0]):
        r, c = 4 * (i // 2), 128 * (i % 2)
        shares[i] = grad[r : r + 4, c : c + 128]

    bag, samples = owners.shape
    entries = bag * samples
    width = projection.shape[0]
    slabs, slab_rows, lanes = out.shape
    owner_count = slabs * X

    def flat(ref):
        return jnp.concatenate([ref[k : k + 1, :] for k in range(bag)], axis=1)

    pool_grad = dot(projection[...].astype(LOW), output_grad[...], NT)
    grads = jnp.concatenate(
        [(pool_grad * weights[k : k + 1, :]).astype(LOW) for k in range(bag)], axis=1
    )
    owner, row = flat(owners), flat(rows)
    hits = jnp.where(iota((owner_count, entries), 0) == owner, 1.0, 0.0)
    before = jnp.where(iota((entries, entries), 0) < iota((entries, entries), 1), 1.0, 0.0)
    earlier = jnp.dot(hits.astype(LOW), before.astype(LOW), preferred_element_type=FULL)
    rank = jnp.sum(hits * earlier, axis=0, keepdims=True).astype(jnp.int32)
    odd = rank & 1
    base = owner * QUAD
    pair_at = base + (rank >> 1)
    place = iota((slabs * slab_rows, entries), 0)

    def chosen(at):
        return jnp.where(place == at, 1.0, 0.0).astype(LOW)

    picks = jnp.concatenate(
        [
            chosen(jnp.where(odd == 0, pair_at, -1)),
            chosen(jnp.where(odd == 1, pair_at, -1)),
            chosen(base + (QUAD - 1)),
        ],
        axis=1,
    )
    blank = jnp.zeros((width, entries), LOW)
    lane = iota((lanes, entries), 0)
    numbers = jnp.where(lane == 2 * rank, row >> 8, 0) + jnp.where(
        lane == 2 * rank + 1, row & 255, 0
    )
    values = jnp.concatenate(
        [
            jnp.concatenate([grads, blank], axis=0),
            jnp.concatenate([blank, grads], axis=0),
            numbers.astype(FULL).astype(LOW),
        ],
        axis=1,
    )
    sent = dot(picks, values, NT).astype(LOW)
    for i in range(slabs):
        out[(i + slabs // 2) % slabs] = sent[i * slab_rows : (i + 1) * slab_rows, :]


def join_kernel(sent, shares, out):
    slabs, slab_rows, _ = sent.shape
    share = halves(jnp.sum(shares[...], axis=0)).astype(LOW)
    for i in range(slabs):
        out[i, 0:slab_rows, :] = sent[i]
        out[i, slab_rows:, :] = share


def regroup_kernel(got, out):
    slabs, _, lanes = got.shape
    width = lanes // 2
    slab_rows = X * QUAD
    copies = out.shape[0] // X
    count = slabs * slab_rows
    flat = got[:, 0:slab_rows, :].reshape(count, lanes)

    def source(lane, pairs, first):
        block = 2 * pairs * slabs
        within = lane % block
        pair = (within // slabs) % pairs + first
        return (within % slabs) * slab_rows + (lane // block) * QUAD, pair, within // (
            slabs * pairs
        )

    def turned(pairs, first):
        size = X * 2 * pairs * slabs
        lane = iota((count, size), 1)
        row = iota((count, size), 0)
        slab, pair, odd = source(lane, pairs, first)
        at = slab + pair
        even_move = jnp.where((row == at) & (odd == 0), 1.0, 0.0).astype(LOW)
        odd_move = jnp.where((row == at) & (odd == 1), 1.0, 0.0).astype(LOW)
        move = jnp.where(row == slab + (QUAD - 1), 1.0, 0.0).astype(LOW)
        data = dot(flat[:, 0:width], even_move, TN) + dot(flat[:, width:], odd_move, TN)
        spread = dot(flat, move, TN)[0:16, :]
        down = iota((16, size), 0)
        _, pair, odd = source(iota((16, size), 1), pairs, first)
        slot = 2 * (2 * pair + odd)
        high = jnp.sum(jnp.where(down == slot, spread, 0.0), axis=0, keepdims=True)
        low = jnp.sum(jnp.where(down == slot + 1, spread, 0.0), axis=0, keepdims=True)
        return data.astype(LOW), high, low

    many, many_high, many_low = turned(2, 0)
    few, few_high, few_low = turned(1, 2)
    total = jnp.sum(got[:, slab_rows:, :].astype(FULL), axis=0)
    tail = halves(total[0:4, :] + total[4:8, :])
    blank = jnp.zeros((5, lanes), FULL)
    for x in range(X):
        here = slice(x * lanes, (x + 1) * lanes)
        half = slice(x * width, (x + 1) * width)
        rest = jnp.concatenate([few[0 : width // 2, half], few[width // 2 :, half]], axis=1)
        last = jnp.concatenate(
            [
                many_high[:, here],
                many_low[:, here],
                jnp.concatenate([few_high[:, half], few_low[:, half]], axis=1),
                blank,
                tail,
            ],
            axis=0,
        ).astype(LOW)
        for j in range(copies):
            out[x * copies + j, 0:width, :] = many[:, here]
            out[x * copies + j, width : width + width // 2, :] = rest
            out[x * copies + j, width + width // 2 :, :] = last


def update_kernel(
    got,
    table,
    state,
    projection,
    projection_state,
    new_table,
    new_state,
    new_projection,
    new_projection_state,
    spread,
    marks,
    total,
    grad,
    *,
    group,
):
    reps, peers, rows, lanes = got.shape
    width, table_rows = table.shape
    half = width // 2
    low_count = 256
    high_count = table_rows // low_count
    marked = iota((low_count, lanes), 0).astype(FULL).astype(LOW)

    def put(at, entry, high, low):
        cols = slice(at, at + lanes)
        high = jnp.broadcast_to(high, (width, lanes)).astype(LOW)
        low = jnp.broadcast_to(low, (low_count, lanes)).astype(LOW)
        for h in range(high_count):
            spread[h * width : (h + 1) * width, cols] = jnp.where(
                high == h, entry, jnp.zeros_like(entry)
            )
        marks[:, cols] = jnp.where(low == marked, 1.0, 0.0).astype(LOW)

    def beside(a, b):
        first = jnp.concatenate([a[:, 0:width], b[:, 0:width]], axis=1)
        second = jnp.concatenate([a[:, width:], b[:, width:]], axis=1)
        return first, second

    for first in range(0, peers, group):
        at = 0
        for n in range(first, first + group):
            pair = [got.at[r, n] for r in range(reps)]
            numbers = [block[width + half : rows, :].astype(FULL) for block in pair]
            for block, number in zip(pair, numbers, strict=True):
                put(at, block[0:width, :], number[0:1, :], number[1:2, :])
                at += lanes
            top, bottom = beside(*[block[width : width + half, :] for block in pair])
            high, low = beside(*[number[2:3, :] for number in numbers])
            put(at, jnp.concatenate([top, bottom], axis=0), high, low)
            at += lanes
        part = dot(spread[...], marks[...], NT)
        if first == 0:
            total[...] = part
        else:
            total[...] += part

    for h in range(high_count):
        cols = slice(h * low_count, (h + 1) * low_count)
        dense = total[h * width : (h + 1) * width, :]
        fresh = state[:, cols] + jnp.sum(dense * dense, axis=0, keepdims=True) * (1.0 / width)
        new_state[:, cols] = fresh
        new_table[:, cols] = table[:, cols] - learn_rate * dense / (jnp.sqrt(fresh) + epsilon)

    for i in range(reps * peers):
        r, c = 4 * (i // 2), 128 * (i % 2)
        tail = got[i % reps, i // reps, width + half : rows, :].astype(FULL)
        grad[r : r + 4, c : c + 128] = tail[8:12, :] + tail[12:16, :]
    whole = grad[...]
    fresh = projection_state[...] + whole * whole
    new_projection_state[...] = fresh
    new_projection[...] = projection[...] - learn_rate * whole / (jnp.sqrt(fresh) + epsilon)


def call(kernel, outs, *args, scratch=(), where=pltpu.VMEM):
    spec = pl.BlockSpec(memory_space=pltpu.VMEM)
    return pl.pallas_call(
        kernel,
        out_shape=outs,
        in_specs=[pl.BlockSpec(memory_space=where)] * len(args),
        out_specs=jax.tree.map(lambda _: spec, outs),
        scratch_shapes=list(scratch),
        compiler_params=pltpu.CompilerParams(vmem_limit_bytes=40 * 2**20),
    )(*args)


def shards(
    output_grad,
    pooled,
    bag_owners,
    bag_rows,
    bag_weights,
    embed_table,
    table_state,
    projection,
    projection_state,
):
    depth = lax.axis_size("z")
    peers = lax.axis_size(PLANE)
    reps = lax.axis_size("rep")
    table_rows, width = embed_table.shape
    lanes = 2 * width

    with jax.named_scope("route"):
        inputs = (
            output_grad,
            pooled.T,
            projection,
            bag_owners.T,
            bag_rows.T,
            bag_weights.T,
        )
        shares, sent = call(
            route_kernel,
            (
                jax.ShapeDtypeStruct((peers, 4, 128), FULL),
                jax.ShapeDtypeStruct((depth, X * QUAD, lanes), LOW),
            ),
            *inputs,
            scratch=[pltpu.VMEM(a.shape, a.dtype) for a in inputs]
            + [pltpu.SemaphoreType.DMA((len(inputs),))],
            where=pltpu.HBM,
        )
    with jax.named_scope("weight_plane"):
        shares = lax.all_to_all(shares, PLANE, 0, 0, tiled=True)
    with jax.named_scope("join"):
        sent = call(
            join_kernel,
            jax.ShapeDtypeStruct((depth, X * QUAD + 8, lanes), LOW),
            sent,
            shares,
        )
    ring = [[(i + depth // 2) % depth for i in range(depth)]]
    with jax.named_scope("along_z"):
        got = lax.all_to_all(sent, "z", 0, 0, axis_index_groups=ring, tiled=True)
    with jax.named_scope("regroup"):
        sent = call(
            regroup_kernel,
            jax.ShapeDtypeStruct((peers // reps, width + width // 2 + 16, lanes), LOW),
            got,
        )
    with jax.named_scope("in_plane"):
        got = lax.all_to_all(sent, ("x", "col"), 0, 0, tiled=True)
    with jax.named_scope("on_chip"):
        got = lax.all_gather(got, "rep")
    with jax.named_scope("update"):
        group = 4
        columns = group * (reps + 1) * lanes
        new_table, new_state, new_projection, new_projection_state = call(
            functools.partial(update_kernel, group=group),
            (
                jax.ShapeDtypeStruct((width, table_rows), FULL),
                jax.ShapeDtypeStruct((1, table_rows), FULL),
                jax.ShapeDtypeStruct(projection.shape, FULL),
                jax.ShapeDtypeStruct(projection.shape, FULL),
            ),
            got,
            embed_table.T,
            table_state.reshape(1, table_rows),
            projection,
            projection_state,
            scratch=(
                pltpu.VMEM((table_rows // 256 * width, columns), LOW),
                pltpu.VMEM((256, columns), LOW),
                pltpu.VMEM((table_rows // 256 * width, 256), FULL),
                pltpu.VMEM(projection.shape, FULL),
            ),
        )
    return (
        new_table.T,
        new_state.reshape(table_rows),
        new_projection,
        new_projection_state,
    )


def solution(mesh):
    sizes = mesh.shape
    fine = Mesh(
        mesh.devices.reshape(sizes["row"] // X, X, sizes["col"], sizes["rep"]),
        ("z", "x", "col", "rep"),
    )
    split = P(("z", "x", "col", "rep"), None)
    owned = ("z", "x")
    return jax.shard_map(
        shards,
        mesh=fine,
        in_specs=(split,) * 5 + (P(owned, None), P(owned), P(), P()),
        out_specs=(P(owned, None), P(owned), P(), P()),
        check_vma=False,
    )
```

time: 1030 us -> 98.3 us (0.10)
  waiting for transfers between devices: 943 us -> 0 us
  blocking collectives: 0 us -> 84.9 us
  starting transfers between devices: 42.1 us -> 0 us
  other arithmetic: 19.3 us -> 0 us
  between operations: 14.3 us -> 0.7 us
    psum x2 -> x0, waiting for transfers between devices: 903 us -> none  [the longest x1 818 us: shards(): total_grad = lax.psum(weight_grad, ('row', 'col', 'rep'))]
    all_to_all x0 -> x3, blocking collectives: none -> 79.7 us  [the longest x1 43.9 us: shards(): got = lax.all_to_all(sent, 'z', 0, 0, axis_index_groups=ring, tiled=True)]
    all_to_all x2 -> x0, starting transfers between devices: 41.8 us -> none  [the longest x1 33.6 us: shards(): lax.all_to_all(send_ids, 'row', split_axis=0, concat_axis=0, tiled=True)]
    all_to_all x2 -> x0, waiting for transfers between devices: 40.6 us -> none  [the longest x1 22.5 us: shards(): lax.all_to_all(send_rows, 'row', split_axis=0, concat_axis=0, tiled=True)]
  transfers between devices with their start and end apart: 4 -> 0, of which waited for: 4 -> 0; matrix products, arithmetic and copies ran while one was open for 2% -> 0% of each run, Pallas kernels for 0% -> 0%
where the time goes in v1:
time: 98.3 us; the launch traced here: 97.9 us
  blocking collectives  84.9 us (86%)
  Pallas kernels  9.2 us (9%)
  local copies, waits for them, and re-layouts  3.1 us (3%)
    all_to_all x1, blocking collectives, shards(): got = lax.all_to_all(sent, 'z', 0, 0, axis_index_groups=ring, tiled=True)  43.9 us
    all_to_all x1, blocking collectives, shards(): shares = lax.all_to_all(shares, PLANE, 0, 0, tiled=True)  24.3 us
    all_to_all x1, blocking collectives, shards(): got = lax.all_to_all(sent, ('x', 'col'), 0, 0, tiled=True)  11.5 us
    pallas_call x4, Pallas kernels, call(): pl.pallas_call(kernel, out_shape=outs, in_specs=[pl.BlockSpec(memory_spac...  9.2 us
    all_gather x1, blocking collectives, shards(): got = lax.all_gather(got, 'rep')  5.24 us
    unnamed x20, local copies, waits for them, and re-layouts  3.1 us

profile of v1, /device:TPU:1, one launch (start us, length us, event | category | flops | bytes accessed | tf_op | source)
XLA Modules:
  0.0 97.9 jit_solution(9762113609685509889)
XLA Ops:
  0.6 0.0 copy-start.9
  0.6 0.0 copy-start.8
  0.7 0.0 copy-start.7
  0.7 0.7 copy-done.9
  1.3 0.0 copy-done.8
  1.3 0.0 copy-done.7
  1.3 0.0 copy-start.1
  1.3 0.8 copy-done.1
  2.2 0.0 copy-start.4
  2.2 0.8 copy-done.4
  3.0 0.0 copy-start.6
  3.0 0.7 copy-done.6
  3.7 1.1 %route.1 = (f32[32,4,128]{2,1,0:T(4,128)S(1)}, bf16[32,16,128]{2,1,0:T(8,128)(2,1)S(1)}) custom-call(bf16[128,256]{1,0:T(8,128)(2,1)S(1)} %copy-done.4, bf16[64,128]{1,0:T(8,128)(2,1)S(1)} %bitcast.12, f32[64,256]{1,0:T(8,128)S(1)} %copy-done.1, s32[4,128]{1,0:T(4,128)S(1)} %bitcast.13, s32[4,128]{1,0:T(4,128)S(1)} %bitcast.14, f32[4,128]{1,0:T(4,128)S(1)} %bitcast.15), custom_call_target="tpu_custom_call" | custom-call | tf_op jit(solution)/shard_map/route/pallas_call | solution.py:250
  4.8 24.3 %all_to_all.15.shares = f32[32,4,128]{2,1,0:T(4,128)S(1)} all-to-all(f32[32,4,128]{2,1,0:T(4,128)S(1)} %get-tuple-element.11), channel_id=1, replica_groups=mesh['z'=32,'x'=4,'col'=4,'rep'=2] {'x','col','rep'}, dimensions={0} | all-to-all | bytes 131072 | tf_op jit(solution)/shard_map/weight_plane/all_to_all | solution.py:298
  29.1 43.9 %all_to_all.16.got = bf16[32,24,128]{2,1,0:T(8,128)(2,1)S(1)} all-to-all(bf16[32,24,128]{2,1,0:T(8,128)(2,1)S(1)} %join.1), channel_id=1, replica_groups={{512,544,576,608,640,672,704,736,768,800,832,864,896,928,960,992,0,32,6..., dimensions={0} | all-to-all | bytes 393216 | tf_op jit(solution)/shard_map/along_z/all_to_all | solution.py:308
  73.0 0.8 regroup.1
  73.8 0.0 copy-start
  73.8 11.5 %all_to_all.17 = bf16[16,112,128]{2,1,0:T(8,128)(2,1)S(1)} all-to-all(bf16[16,112,128]{2,1,0:T(8,128)(2,1)S(1)} %regroup.1), channel_id=1, replica_groups=mesh['z'=32,'x'=4,'col'=4,'rep'=2] {'x','col'}, dimensions={0} | all-to-all | bytes 917504 | tf_op jit(solution)/shard_map/in_plane/all_to_all | solution.py:316
  85.3 5.2 %all-gather = bf16[32,112,128]{2,1,0:T(8,128)(2,1)S(1)} all-gather(bf16[16,112,128]{2,1,0:T(8,128)(2,1)S(1)} %all_to_all.17), channel_id=2, replica_groups=mesh['z'=32,'x'=4,'col'=4,'rep'=2] {'rep'}, dimensions={0}, use_global_device_ids=true | all-gather | bytes 1376256 | tf_op jit(solution)/shard_map/on_chip/all_gather | solution.py:318
  90.6 0.0 copy-done
  90.6 0.0 copy-done.2
  90.6 0.0 copy-done.3
  90.6 0.0 copy-done.5
  90.6 7.3 %update.1 = (f32[64,4096]{1,0:T(8,128)}, f32[1,4096]{1,0:T(1,128)}, f32[64,256]{1,0:T(8,128)}, f32[64,256]{1,0:T(8,128)}) custom-call(bf16[2,16,112,128]{3,2,1,0:T(8,128)(2,1)S(1)} %bitcast.9, f32[64,4096]{1,0:T(8,128)S(1)} %bitcast.10, f32[1,4096]{1,0:T(1,128)S(1)} %bitcast.11, f32[64,256]{1,0:T(8,128)S(1)} %copy-done.2, f32[64,256]{1,0:T(8,128)S(1)} %copy-done.3), custom_call_target="tpu_custom_call" | custom-call | tf_op jit(solution)/shard_map/update/pallas_call | solution.py:250
  (4 shorter events, 0.1 us)
Async XLA Ops:
  0.6 0.7 copy-start.9
  0.6 0.7 copy-start.8
  0.7 0.7 copy-start.7
  1.3 0.8 copy-start.1
  2.2 0.8 copy-start.4
  3.0 0.7 copy-start.6
  73.8 16.8 %copy-start = (f32[4096,64]{0,1:T(8,128)S(1)}, f32[4096,64]{0,1:T(8,128)}, u32[]{:S(2)}) copy-start(f32[4096,64]{0,1:T(8,128)} %param.14) | copy-start | bytes 3145732
  85.3 5.2 %copy-start.2 = (f32[64,256]{1,0:T(8,128)S(1)}, f32[64,256]{1,0:T(8,128)}, u32[]{:S(2)}) copy-start(f32[64,256]{1,0:T(8,128)} %projection.1) | copy-start | bytes 196612
  85.3 5.2 %copy-start.3 = (f32[64,256]{1,0:T(8,128)S(1)}, f32[64,256]{1,0:T(8,128)}, u32[]{:S(2)}) copy-start(f32[64,256]{1,0:T(8,128)} %projection_state.1) | copy-start | bytes 196612
  85.3 5.2 %copy-start.5 = (f32[4096]{0:T(1024)S(1)}, f32[4096]{0:T(1024)}, u32[]{:S(2)}) copy-start(f32[4096]{0:T(1024)} %param.15) | copy-start | bytes 49156

commit v2 on v1

--- a/solution.py
+++ b/solution.py
@@ -1,5 +1,3 @@
-import functools
-
 import jax
 import jax.numpy as jnp
 from jax import lax
@@ -13,6 +11,7 @@
 
 X = 4
 CAP = 6
+STEP = 16
 QUAD = 4
 PLANE = ("x", "col", "rep")
 LOW = jnp.bfloat16
@@ -185,55 +184,55 @@
     marks,
     total,
     grad,
-    *,
-    group,
 ):
     reps, peers, rows, lanes = got.shape
     width, table_rows = table.shape
     half = width // 2
-    low_count = 256
+    low_count = marks.shape[0]
     high_count = table_rows // low_count
-    marked = iota((low_count, lanes), 0).astype(FULL).astype(LOW)
+    marked = iota((STEP, lanes), 0).astype(FULL).astype(LOW)
+    none = jnp.zeros((STEP, lanes), LOW)
+    one = jnp.ones((STEP, lanes), LOW)
 
     def put(at, entry, high, low):
         cols = slice(at, at + lanes)
-        high = jnp.broadcast_to(high, (width, lanes)).astype(LOW)
-        low = jnp.broadcast_to(low, (low_count, lanes)).astype(LOW)
+        high = jnp.broadcast_to(high, (STEP, lanes)).astype(LOW)
+        low = jnp.broadcast_to(low, (STEP, lanes))
         for h in range(high_count):
-            spread[h * width : (h + 1) * width, cols] = jnp.where(
-                high == h, entry, jnp.zeros_like(entry)
+            here = high == jnp.full((STEP, lanes), h, LOW)
+            for r in range(0, width, STEP):
+                spread[h * width + r : h * width + r + STEP, cols] = jnp.where(
+                    here, entry[r : r + STEP, :], none
+                )
+        for r in range(0, low_count, STEP):
+            marks[r : r + STEP, cols] = jnp.where(
+                (low - float(r)).astype(LOW) == marked, one, none
             )
-        marks[:, cols] = jnp.where(low == marked, 1.0, 0.0).astype(LOW)
 
     def beside(a, b):
         first = jnp.concatenate([a[:, 0:width], b[:, 0:width]], axis=1)
         second = jnp.concatenate([a[:, width:], b[:, width:]], axis=1)
         return first, second
 
-    for first in range(0, peers, group):
-        at = 0
-        for n in range(first, first + group):
-            pair = [got.at[r, n] for r in range(reps)]
-            numbers = [block[width + half : rows, :].astype(FULL) for block in pair]
-            for block, number in zip(pair, numbers, strict=True):
-                put(at, block[0:width, :], number[0:1, :], number[1:2, :])
-                at += lanes
-            top, bottom = beside(*[block[width : width + half, :] for block in pair])
-            high, low = beside(*[number[2:3, :] for number in numbers])
-            put(at, jnp.concatenate([top, bottom], axis=0), high, low)
+    at = 0
+    for n in range(peers):
+        pair = [got.at[r, n] for r in range(reps)]
+        numbers = [block[width + half : rows, :].astype(FULL) for block in pair]
+        for block, number in zip(pair, numbers, strict=True):
+            put(at, block[0:width, :], number[0:1, :], number[1:2, :])
             at += lanes
-        part = dot(spread[...], marks[...], NT)
-        if first == 0:
-            total[...] = part
-        else:
-            total[...] += part
+        top, bottom = beside(*[block[width : width + half, :] for block in pair])
+        high, low = beside(*[number[2:3, :] for number in numbers])
+        put(at, jnp.concatenate([top, bottom], axis=0), high, low)
+        at += lanes
+    total[...] = dot(spread[...], marks[...], NT)
 
     for h in range(high_count):
         cols = slice(h * low_count, (h + 1) * low_count)
         dense = total[h * width : (h + 1) * width, :]
         fresh = state[:, cols] + jnp.sum(dense * dense, axis=0, keepdims=True) * (1.0 / width)
         new_state[:, cols] = fresh
-        new_table[:, cols] = table[:, cols] - learn_rate * dense / (jnp.sqrt(fresh) + epsilon)
+        new_table[:, cols] = table[:, cols] - dense * (learn_rate / (jnp.sqrt(fresh) + epsilon))
 
     for i in range(reps * peers):
         r, c = 4 * (i // 2), 128 * (i % 2)
@@ -245,7 +244,7 @@
     new_projection[...] = projection[...] - learn_rate * whole / (jnp.sqrt(fresh) + epsilon)
 
 
-def call(kernel, outs, *args, scratch=(), where=pltpu.VMEM):
+def call(kernel, outs, *args, scratch=(), where=pltpu.VMEM, limit=40 * 2**20):
     spec = pl.BlockSpec(memory_space=pltpu.VMEM)
     return pl.pallas_call(
         kernel,
@@ -253,7 +252,7 @@
         in_specs=[pl.BlockSpec(memory_space=where)] * len(args),
         out_specs=jax.tree.map(lambda _: spec, outs),
         scratch_shapes=list(scratch),
-        compiler_params=pltpu.CompilerParams(vmem_limit_bytes=40 * 2**20),
+        compiler_params=pltpu.CompilerParams(vmem_limit_bytes=limit),
     )(*args)
 
 
@@ -293,6 +292,7 @@
             scratch=[pltpu.VMEM(a.shape, a.dtype) for a in inputs]
             + [pltpu.SemaphoreType.DMA((len(inputs),))],
             where=pltpu.HBM,
+            limit=60 * 2**20,
         )
     with jax.named_scope("weight_plane"):
         shares = lax.all_to_all(shares, PLANE, 0, 0, tiled=True)
@@ -317,10 +317,9 @@
     with jax.named_scope("on_chip"):
         got = lax.all_gather(got, "rep")
     with jax.named_scope("update"):
-        group = 4
-        columns = group * (reps + 1) * lanes
+        columns = peers // 2 * 3 * lanes
         new_table, new_state, new_projection, new_projection_state = call(
-            functools.partial(update_kernel, group=group),
+            update_kernel,
             (
                 jax.ShapeDtypeStruct((width, table_rows), FULL),
                 jax.ShapeDtypeStruct((1, table_rows), FULL),

time: 98.3 us -> 94.5 us (0.961)
  local copies, waits for them, and re-layouts: 3.1 us -> 0.02 us
    unnamed x20 -> x10, local copies, waits for them, and re-layouts: 3.1 us -> 0.02 us
    all_to_all x1, blocking collectives: 24.3 us -> 25.3 us  [shards(): shares = lax.all_to_all(shares, PLANE, 0, 0, tiled=True)]
where the time goes in v2:
time: 94.5 us; the launch traced here: 94.2 us
  blocking collectives  85.2 us (90%)
  Pallas kernels  8.24 us (9%)
    all_to_all x1, blocking collectives, shards(): got = lax.all_to_all(sent, 'z', 0, 0, axis_index_groups=ring, tiled=True)  43.2 us
    all_to_all x1, blocking collectives, shards(): shares = lax.all_to_all(shares, PLANE, 0, 0, tiled=True)  25.3 us
    all_to_all x1, blocking collectives, shards(): got = lax.all_to_all(sent, ('x', 'col'), 0, 0, tiled=True)  11.5 us
    pallas_call x4, Pallas kernels, call(): pl.pallas_call(kernel, out_shape=outs, in_specs=[pl.BlockSpec(memory_spac...  8.24 us
    all_gather x1, blocking collectives, shards(): got = lax.all_gather(got, 'rep')  5.24 us

profile of v2, /device:TPU:1, one launch (start us, length us, event | category | flops | bytes accessed | tf_op | source)
XLA Modules:
  0.0 94.2 jit_solution(1356131623830904568)
XLA Ops:
  0.6 2.5 %route.1 = (f32[32,4,128]{2,1,0:T(4,128)}, bf16[32,16,128]{2,1,0:T(8,128)(2,1)}) custom-call(bf16[128,256]{1,0:T(8,128)(2,1)} %refs_0_.1, bf16[64,128]{1,0:T(8,128)(2,1)} %bitcast.12, f32[64,256]{1,0:T(8,128)} %projection.1, s32[4,128]{1,0:T(4,128)} %bitcast.13, s32[4,128]{1,0:T(4,128)} %bitcast.14, f32[4,128]{1,0:T(4,128)} %bitcast.15), custom_call_target="tpu_custom_call" | custom-call | tf_op jit(solution)/shard_map/route/pallas_call | solution.py:249
  3.1 0.0 copy-start.2
  3.1 25.3 %all_to_all.15.shares = f32[32,4,128]{2,1,0:T(4,128)S(1)} all-to-all(f32[32,4,128]{2,1,0:T(4,128)} %get-tuple-element.11), channel_id=1, replica_groups=mesh['z'=32,'x'=4,'col'=4,'rep'=2] {'x','col','rep'}, dimensions={0} | all-to-all | bytes 131072 | tf_op jit(solution)/shard_map/weight_plane/all_to_all | solution.py:298
  28.4 0.0 copy-done.2
  28.4 43.2 %all_to_all.16.got = bf16[32,24,128]{2,1,0:T(8,128)(2,1)S(1)} all-to-all(bf16[32,24,128]{2,1,0:T(8,128)(2,1)S(1)} %join.1), channel_id=1, replica_groups={{512,544,576,608,640,672,704,736,768,800,832,864,896,928,960,992,0,32,6..., dimensions={0} | all-to-all | bytes 393216 | tf_op jit(solution)/shard_map/along_z/all_to_all | solution.py:308
  71.6 0.8 regroup.1
  72.4 0.0 copy-start
  72.4 11.5 %all_to_all.17 = bf16[16,112,128]{2,1,0:T(8,128)(2,1)S(1)} all-to-all(bf16[16,112,128]{2,1,0:T(8,128)(2,1)S(1)} %regroup.1), channel_id=1, replica_groups=mesh['z'=32,'x'=4,'col'=4,'rep'=2] {'x','col'}, dimensions={0} | all-to-all | bytes 917504 | tf_op jit(solution)/shard_map/in_plane/all_to_all | solution.py:316
  83.9 0.0 copy-start.1
  83.9 0.0 copy-start.3
  84.0 0.0 copy-start.4
  84.0 5.2 %all-gather = bf16[32,112,128]{2,1,0:T(8,128)(2,1)S(1)} all-gather(bf16[16,112,128]{2,1,0:T(8,128)(2,1)S(1)} %all_to_all.17), channel_id=2, replica_groups=mesh['z'=32,'x'=4,'col'=4,'rep'=2] {'rep'}, dimensions={0}, use_global_device_ids=true | all-gather | bytes 1376256 | tf_op jit(solution)/shard_map/on_chip/all_gather | solution.py:318
  89.2 0.0 copy-done
  89.2 0.0 copy-done.1
  89.2 0.0 copy-done.3
  89.2 0.0 copy-done.4
  89.2 5.0 %update.1 = (f32[64,4096]{1,0:T(8,128)}, f32[1,4096]{1,0:T(1,128)}, f32[64,256]{1,0:T(8,128)}, f32[64,256]{1,0:T(8,128)}) custom-call(bf16[2,16,112,128]{3,2,1,0:T(8,128)(2,1)S(1)} %bitcast.9, f32[64,4096]{1,0:T(8,128)S(1)} %bitcast.10, f32[1,4096]{1,0:T(1,128)S(1)} %bitcast.11, f32[64,256]{1,0:T(8,128)S(1)} %copy-done.1, f32[64,256]{1,0:T(8,128)S(1)} %copy-done.3), custom_call_target="tpu_custom_call" | custom-call | tf_op jit(solution)/shard_map/update/pallas_call | solution.py:249
  (1 shorter events, 0.0 us)
Async XLA Ops:
  3.1 25.3 %copy-start.2 = (bf16[32,16,128]{2,1,0:T(8,128)(2,1)S(1)}, bf16[32,16,128]{2,1,0:T(8,128)(2,1)}, u32[]{:S(2)}) copy-start(bf16[32,16,128]{2,1,0:T(8,128)(2,1)} %get-tuple-element.10.sent) | copy-start | bytes 393220
  72.4 16.8 %copy-start = (f32[4096,64]{0,1:T(8,128)S(1)}, f32[4096,64]{0,1:T(8,128)}, u32[]{:S(2)}) copy-start(f32[4096,64]{0,1:T(8,128)} %param.14) | copy-start | bytes 3145732
  83.9 5.2 %copy-start.1 = (f32[64,256]{1,0:T(8,128)S(1)}, f32[64,256]{1,0:T(8,128)}, u32[]{:S(2)}) copy-start(f32[64,256]{1,0:T(8,128)} %projection.1) | copy-start | bytes 196612
  83.9 5.2 %copy-start.3 = (f32[64,256]{1,0:T(8,128)S(1)}, f32[64,256]{1,0:T(8,128)}, u32[]{:S(2)}) copy-start(f32[64,256]{1,0:T(8,128)} %projection_state.1) | copy-start | bytes 196612
  84.0 5.2 %copy-start.4 = (f32[4096]{0:T(1024)S(1)}, f32[4096]{0:T(1024)}, u32[]{:S(2)}) copy-start(f32[4096]{0:T(1024)} %param.15) | copy-start | bytes 49156

commit v3 on v2

--- a/solution.py
+++ b/solution.py
@@ -1,3 +1,5 @@
+import functools
+
 import jax
 import jax.numpy as jnp
 from jax import lax
@@ -10,6 +12,9 @@
 epsilon = 1e-06
 
 X = 4
+Z_FIRST = 18
+SHARE_FIRST = (3, 3)
+ROWS_FIRST = (2, 2)
 CAP = 6
 STEP = 16
 QUAD = 4
@@ -100,7 +105,7 @@
     )
     sent = dot(picks, values, NT).astype(LOW)
     for i in range(slabs):
-        out[(i + slabs // 2) % slabs] = sent[i * slab_rows : (i + 1) * slab_rows, :]
+        out[(i - Z_FIRST) % slabs] = sent[i * slab_rows : (i + 1) * slab_rows, :]
 
 
 def join_kernel(sent, shares, out):
@@ -111,11 +116,11 @@
         out[i, slab_rows:, :] = share
 
 
-def regroup_kernel(got, out):
+def regroup_kernel(got, out, *, order):
     slabs, _, lanes = got.shape
     width = lanes // 2
     slab_rows = X * QUAD
-    copies = out.shape[0] // X
+    copies = len(order) // X
     count = slabs * slab_rows
     flat = got[:, 0:slab_rows, :].reshape(count, lanes)
 
@@ -164,10 +169,11 @@
             ],
             axis=0,
         ).astype(LOW)
-        for j in range(copies):
-            out[x * copies + j, 0:width, :] = many[:, here]
-            out[x * copies + j, width : width + width // 2, :] = rest
-            out[x * copies + j, width + width // 2 :, :] = last
+        for n, device in enumerate(order):
+            if device // copies == x:
+                out[n, 0:width, :] = many[:, here]
+                out[n, width : width + width // 2, :] = rest
+                out[n, width + width // 2 :, :] = last
 
 
 def update_kernel(
@@ -184,6 +190,8 @@
     marks,
     total,
     grad,
+    *,
+    chunks,
 ):
     reps, peers, rows, lanes = got.shape
     width, table_rows = table.shape
@@ -235,7 +243,8 @@
         new_table[:, cols] = table[:, cols] - dense * (learn_rate / (jnp.sqrt(fresh) + epsilon))
 
     for i in range(reps * peers):
-        r, c = 4 * (i // 2), 128 * (i % 2)
+        k = chunks[i // reps] * reps + i % reps
+        r, c = 4 * (k // 2), 128 * (k % 2)
         tail = got[i % reps, i // reps, width + half : rows, :].astype(FULL)
         grad[r : r + 4, c : c + 128] = tail[8:12, :] + tail[12:16, :]
     whole = grad[...]
@@ -272,6 +281,17 @@
     reps = lax.axis_size("rep")
     table_rows, width = embed_table.shape
     lanes = 2 * width
+    cols = lax.axis_size("col")
+
+    def order(first):
+        return [
+            (x + first[0]) % X * cols + (c + first[1]) % cols
+            for x in range(X)
+            for c in range(cols)
+        ]
+
+    share_order, rows_order = order(SHARE_FIRST), order(ROWS_FIRST)
+    share_group = [[d * reps + r for d in share_order for r in range(reps)]]
 
     with jax.named_scope("route"):
         inputs = (
@@ -295,7 +315,9 @@
             limit=60 * 2**20,
         )
     with jax.named_scope("weight_plane"):
-        shares = lax.all_to_all(shares, PLANE, 0, 0, tiled=True)
+        shares = lax.all_to_all(
+            shares, PLANE, 0, 0, axis_index_groups=share_group, tiled=True
+        )
     with jax.named_scope("join"):
         sent = call(
             join_kernel,
@@ -303,23 +325,27 @@
             sent,
             shares,
         )
-    ring = [[(i + depth // 2) % depth for i in range(depth)]]
+    ring = [[(i + Z_FIRST) % depth for i in range(depth)]]
     with jax.named_scope("along_z"):
         got = lax.all_to_all(sent, "z", 0, 0, axis_index_groups=ring, tiled=True)
     with jax.named_scope("regroup"):
         sent = call(
-            regroup_kernel,
+            functools.partial(regroup_kernel, order=rows_order),
             jax.ShapeDtypeStruct((peers // reps, width + width // 2 + 16, lanes), LOW),
             got,
         )
     with jax.named_scope("in_plane"):
-        got = lax.all_to_all(sent, ("x", "col"), 0, 0, tiled=True)
+        got = lax.all_to_all(
+            sent, ("x", "col"), 0, 0, axis_index_groups=[rows_order], tiled=True
+        )
     with jax.named_scope("on_chip"):
         got = lax.all_gather(got, "rep")
     with jax.named_scope("update"):
         columns = peers // 2 * 3 * lanes
         new_table, new_state, new_projection, new_projection_state = call(
-            update_kernel,
+            functools.partial(
+                update_kernel, chunks=[share_order.index(d) for d in rows_order]
+            ),
             (
                 jax.ShapeDtypeStruct((width, table_rows), FULL),
                 jax.ShapeDtypeStruct((1, table_rows), FULL),

time: 94.5 us -> 91.2 us (0.965)
  blocking collectives: 85.2 us -> 81.9 us
    all_to_all x1, blocking collectives: 43.2 us -> 41 us  [shards(): got = lax.all_to_all(sent, 'z', 0, 0, axis_index_groups=ring, tiled=True)]
    all_to_all x2, blocking collectives: 36.8 us -> 35.7 us  [the longest x1 24.9 us: shards(): lax.all_to_all(shares, PLANE, 0, 0, axis_index_groups=share_group, tiled=...]
where the time goes in v3:
time: 91.2 us; the launch traced here: 90.9 us
  blocking collectives  81.9 us (90%)
  Pallas kernels  8.24 us (9%)
    all_to_all x1, blocking collectives, shards(): got = lax.all_to_all(sent, 'z', 0, 0, axis_index_groups=ring, tiled=True)  41 us
    all_to_all x1, blocking collectives, shards(): lax.all_to_all(shares, PLANE, 0, 0, axis_index_groups=share_group, tiled=...  24.9 us
    all_to_all x1, blocking collectives, shards(): lax.all_to_all(sent, ('x', 'col'), 0, 0, axis_index_groups=[rows_order],...  10.8 us
    pallas_call x4, Pallas kernels, call(): pl.pallas_call(kernel, out_shape=outs, in_specs=[pl.BlockSpec(memory_spac...  8.24 us
    all_gather x1, blocking collectives, shards(): got = lax.all_gather(got, 'rep')  5.27 us

profile of v3, /device:TPU:1, one launch (start us, length us, event | category | flops | bytes accessed | tf_op | source)
XLA Modules:
  0.0 90.9 jit_solution(13903334923077929174)
XLA Ops:
  0.6 2.5 %route.1 = (f32[32,4,128]{2,1,0:T(4,128)}, bf16[32,16,128]{2,1,0:T(8,128)(2,1)}) custom-call(bf16[128,256]{1,0:T(8,128)(2,1)} %refs_0_.1, bf16[64,128]{1,0:T(8,128)(2,1)} %bitcast.12, f32[64,256]{1,0:T(8,128)} %projection.1, s32[4,128]{1,0:T(4,128)} %bitcast.13, s32[4,128]{1,0:T(4,128)} %bitcast.14, f32[4,128]{1,0:T(4,128)} %bitcast.15), custom_call_target="tpu_custom_call" | custom-call | tf_op jit(solution)/shard_map/route/pallas_call | solution.py:258
  3.1 0.0 copy-start.2
  3.1 24.9 %all_to_all.15.shares = f32[32,4,128]{2,1,0:T(4,128)S(1)} all-to-all(f32[32,4,128]{2,1,0:T(4,128)} %get-tuple-element.11), channel_id=1, replica_groups={{30,31,24,25,26,27,28,29,6,7,0,1,2,3,4,5,14,15,8,9,10,11,12,13,22,23,16..., dimensions={0} | all-to-all | bytes 131072 | tf_op jit(solution)/shard_map/weight_plane/all_to_all | solution.py:318
  28.0 0.0 copy-done.2
  28.1 41.0 %all_to_all.16.got = bf16[32,24,128]{2,1,0:T(8,128)(2,1)S(1)} all-to-all(bf16[32,24,128]{2,1,0:T(8,128)(2,1)S(1)} %join.1), channel_id=1, replica_groups={{576,608,640,672,704,736,768,800,832,864,896,928,960,992,0,32,64,96,128..., dimensions={0} | all-to-all | bytes 393216 | tf_op jit(solution)/shard_map/along_z/all_to_all | solution.py:330
  69.0 0.8 regroup.1
  69.8 0.0 copy-start
  69.8 10.8 %all_to_all.17 = bf16[16,112,128]{2,1,0:T(8,128)(2,1)S(1)} all-to-all(bf16[16,112,128]{2,1,0:T(8,128)(2,1)S(1)} %regroup.1), channel_id=1, replica_groups={{20,22,16,18,28,30,24,26,4,6,0,2,12,14,8,10},{21,23,17,19,29,31,25,27,5..., dimensions={0} | all-to-all | bytes 917504 | tf_op jit(solution)/shard_map/in_plane/all_to_all | solution.py:338
  80.6 0.0 copy-start.1
  80.6 0.0 copy-start.3
  80.6 0.0 copy-start.4
  80.6 5.3 %all-gather = bf16[32,112,128]{2,1,0:T(8,128)(2,1)S(1)} all-gather(bf16[16,112,128]{2,1,0:T(8,128)(2,1)S(1)} %all_to_all.17), channel_id=2, replica_groups=mesh['z'=32,'x'=4,'col'=4,'rep'=2] {'rep'}, dimensions={0}, use_global_device_ids=true | all-gather | bytes 1376256 | tf_op jit(solution)/shard_map/on_chip/all_gather | solution.py:342
  85.9 0.0 copy-done
  85.9 0.0 copy-done.1
  85.9 0.0 copy-done.3
  85.9 0.0 copy-done.4
  85.9 5.0 %update.1 = (f32[64,4096]{1,0:T(8,128)}, f32[1,4096]{1,0:T(1,128)}, f32[64,256]{1,0:T(8,128)}, f32[64,256]{1,0:T(8,128)}) custom-call(bf16[2,16,112,128]{3,2,1,0:T(8,128)(2,1)S(1)} %bitcast.9, f32[64,4096]{1,0:T(8,128)S(1)} %bitcast.10, f32[1,4096]{1,0:T(1,128)S(1)} %bitcast.11, f32[64,256]{1,0:T(8,128)S(1)} %copy-done.1, f32[64,256]{1,0:T(8,128)S(1)} %copy-done.3), custom_call_target="tpu_custom_call" | custom-call | tf_op jit(solution)/shard_map/update/pallas_call | solution.py:258
  (1 shorter events, 0.0 us)
Async XLA Ops:
  3.1 24.9 %copy-start.2 = (bf16[32,16,128]{2,1,0:T(8,128)(2,1)S(1)}, bf16[32,16,128]{2,1,0:T(8,128)(2,1)}, u32[]{:S(2)}) copy-start(bf16[32,16,128]{2,1,0:T(8,128)(2,1)} %get-tuple-element.10.sent) | copy-start | bytes 393220
  69.8 16.1 %copy-start = (f32[4096,64]{0,1:T(8,128)S(1)}, f32[4096,64]{0,1:T(8,128)}, u32[]{:S(2)}) copy-start(f32[4096,64]{0,1:T(8,128)} %param.14) | copy-start | bytes 3145732
  80.6 5.3 %copy-start.1 = (f32[64,256]{1,0:T(8,128)S(1)}, f32[64,256]{1,0:T(8,128)}, u32[]{:S(2)}) copy-start(f32[64,256]{1,0:T(8,128)} %projection.1) | copy-start | bytes 196612
  80.6 5.3 %copy-start.3 = (f32[64,256]{1,0:T(8,128)S(1)}, f32[64,256]{1,0:T(8,128)}, u32[]{:S(2)}) copy-start(f32[64,256]{1,0:T(8,128)} %projection_state.1) | copy-start | bytes 196612
  80.6 5.3 %copy-start.4 = (f32[4096]{0:T(1024)S(1)}, f32[4096]{0:T(1024)}, u32[]{:S(2)}) copy-start(f32[4096]{0:T(1024)} %param.15) | copy-start | bytes 49156

commit v4 on v3

--- a/solution.py
+++ b/solution.py
@@ -39,8 +39,7 @@
     return jnp.concatenate([high, value - high], axis=0)
 
 
-def route_kernel(*refs):
-    ins, outs, held, sems = refs[:6], refs[6:8], refs[8:14], refs[14]
+def fetched(ins, held, sems):
     copies = [
         pltpu.make_async_copy(ins[n], held[n], sems.at[n]) for n in range(len(ins))
     ]
@@ -48,14 +47,18 @@
         copy.start()
     for copy in copies:
         copy.wait()
-    output_grad, pooled_t, projection, owners, rows, weights = held
-    shares, out = outs
-
+    return held
+
+
+def weight_kernel(output_grad, pooled_t, shares, *held):
+    output_grad, pooled_t = fetched((output_grad, pooled_t), held[:-1], held[-1])
     grad = jnp.dot(pooled_t[...], output_grad[...], preferred_element_type=FULL)
     for i in range(shares.shape[0]):
         r, c = 4 * (i // 2), 128 * (i % 2)
         shares[i] = grad[r : r + 4, c : c + 128]
 
+
+def route_kernel(output_grad, projection, owners, rows, weights, out):
     bag, samples = owners.shape
     entries = bag * samples
     width = projection.shape[0]
@@ -134,17 +137,18 @@
 
     def turned(pairs, first):
         size = X * 2 * pairs * slabs
-        lane = iota((count, size), 1)
+        slab, pair, odd = source(iota((1, size), 1), pairs, first)
         row = iota((count, size), 0)
-        slab, pair, odd = source(lane, pairs, first)
-        at = slab + pair
-        even_move = jnp.where((row == at) & (odd == 0), 1.0, 0.0).astype(LOW)
-        odd_move = jnp.where((row == at) & (odd == 1), 1.0, 0.0).astype(LOW)
-        move = jnp.where(row == slab + (QUAD - 1), 1.0, 0.0).astype(LOW)
+
+        def chosen(at):
+            return jnp.where(row == at, 1.0, 0.0).astype(LOW)
+
+        even_move = chosen(jnp.where(odd == 0, slab + pair, -1))
+        odd_move = chosen(jnp.where(odd == 1, slab + pair, -1))
+        move = chosen(slab + (QUAD - 1))
         data = dot(flat[:, 0:width], even_move, TN) + dot(flat[:, width:], odd_move, TN)
         spread = dot(flat, move, TN)[0:16, :]
         down = iota((16, size), 0)
-        _, pair, odd = source(iota((16, size), 1), pairs, first)
         slot = 2 * (2 * pair + odd)
         high = jnp.sum(jnp.where(down == slot, spread, 0.0), axis=0, keepdims=True)
         low = jnp.sum(jnp.where(down == slot + 1, spread, 0.0), axis=0, keepdims=True)
@@ -293,21 +297,11 @@
     share_order, rows_order = order(SHARE_FIRST), order(ROWS_FIRST)
     share_group = [[d * reps + r for d in share_order for r in range(reps)]]
 
-    with jax.named_scope("route"):
-        inputs = (
-            output_grad,
-            pooled.T,
-            projection,
-            bag_owners.T,
-            bag_rows.T,
-            bag_weights.T,
-        )
-        shares, sent = call(
-            route_kernel,
-            (
-                jax.ShapeDtypeStruct((peers, 4, 128), FULL),
-                jax.ShapeDtypeStruct((depth, X * QUAD, lanes), LOW),
-            ),
+    with jax.named_scope("weight"):
+        inputs = (output_grad, pooled.T)
+        shares = call(
+            weight_kernel,
+            jax.ShapeDtypeStruct((peers, 4, 128), FULL),
             *inputs,
             scratch=[pltpu.VMEM(a.shape, a.dtype) for a in inputs]
             + [pltpu.SemaphoreType.DMA((len(inputs),))],
@@ -317,6 +311,16 @@
     with jax.named_scope("weight_plane"):
         shares = lax.all_to_all(
             shares, PLANE, 0, 0, axis_index_groups=share_group, tiled=True
+        )
+    with jax.named_scope("route"):
+        sent = call(
+            route_kernel,
+            jax.ShapeDtypeStruct((depth, X * QUAD, lanes), LOW),
+            output_grad,
+            projection,
+            bag_owners.T,
+            bag_rows.T,
+            bag_weights.T,
         )
     with jax.named_scope("join"):
         sent = call(

time: 91.2 us -> 90.4 us (level)
  blocking collectives: 81.9 us -> 57 us
  starting transfers between devices: 0 us -> 20.7 us
  waiting for transfers between devices: 0 us -> 2.62 us
    all_to_all x1 -> x0, blocking collectives: 24.9 us -> none  [shards(): lax.all_to_all(shares, PLANE, 0, 0, axis_index_groups=share_group, tiled=...]
    all_to_all x0 -> x1, starting transfers between devices: none -> 20.7 us  [shards(): lax.all_to_all(shares, PLANE, 0, 0, axis_index_groups=share_group, tiled=...]
    all_to_all x0 -> x1, waiting for transfers between devices: none -> 2.62 us  [shards(): lax.all_to_all(shares, PLANE, 0, 0, axis_index_groups=share_group, tiled=...]
    pallas_call x4 -> x5, Pallas kernels: 8.24 us -> 8.27 us  [call(): pl.pallas_call(kernel, out_shape=outs, in_specs=[pl.BlockSpec(memory_spac...]
  transfers between devices with their start and end apart: 0 -> 1, of which waited for: 0 -> 1; matrix products, arithmetic and copies ran while one was open for 0% -> 0% of each run, Pallas kernels for 0% -> 1%
where the time goes in v4:
time: 90.4 us; the launch traced here: 90.1 us
  blocking collectives  57 us (63%)
  starting transfers between devices  20.7 us (23%)
  Pallas kernels  8.27 us (9%)
  waiting for transfers between devices  2.62 us (3%)
    all_to_all x1, blocking collectives, shards(): got = lax.all_to_all(sent, 'z', 0, 0, axis_index_groups=ring, tiled=True)  41 us
    all_to_all x1, starting transfers between devices, shards(): lax.all_to_all(shares, PLANE, 0, 0, axis_index_groups=share_group, tiled=...  20.7 us
    all_to_all x1, blocking collectives, shards(): lax.all_to_all(sent, ('x', 'col'), 0, 0, axis_index_groups=[rows_order],...  10.8 us
    pallas_call x5, Pallas kernels, call(): pl.pallas_call(kernel, out_shape=outs, in_specs=[pl.BlockSpec(memory_spac...  8.27 us
    all_gather x1, blocking collectives, shards(): got = lax.all_gather(got, 'rep')  5.27 us
    all_to_all x1, waiting for transfers between devices, shards(): lax.all_to_all(shares, PLANE, 0, 0, axis_index_groups=share_group, tiled=...  2.62 us
  transfers between devices with their start and end apart: 1, of which 1 were waited for; matrix products, arithmetic and copies ran while one was open for 0% of the time, Pallas kernels for 1%

profile of v4, /device:TPU:1, one launch (start us, length us, event | category | flops | bytes accessed | tf_op | source)
XLA Modules:
  0.0 90.1 jit_solution(17327701888814458269)
XLA Ops:
  0.6 0.0 copy-start.7
  0.6 1.6 %weight.1 = f32[32,4,128]{2,1,0:T(4,128)} custom-call(bf16[128,256]{1,0:T(8,128)(2,1)} %output_grad.3, bf16[64,128]{1,0:T(8,128)(2,1)} %bitcast.15), custom_call_target="tpu_custom_call" | custom-call | tf_op jit(solution)/shard_map/weight/pallas_call | solution.py:262
  2.3 0.0 copy-start.1
  2.3 0.0 copy-start.2
  2.3 20.7 %all-to-all-start = ((f32[32,4,128]{2,1,0:T(4,128)}), f32[32,4,128]{2,1,0:T(4,128)S(1)}, u32[]{:S(2)}, u32[]{:S(2)}) async-start(f32[32,4,128]{2,1,0:T(4,128)} %weight.1), calls=%async_computation | async-start | bytes 131072 | tf_op jit(solution)/shard_map/weight_plane/all_to_all | solution.py:312
  23.0 0.0 copy-start.6
  23.0 0.0 copy-start.5
  23.1 0.0 copy-done.7
  23.1 0.0 copy-done.1
  23.1 0.0 copy-done.2
  23.1 0.6 copy-done.6
  23.7 0.0 copy-done.5
  23.7 0.9 route.1.sent
  24.6 2.6 %all-to-all-done.shares = f32[32,4,128]{2,1,0:T(4,128)S(1)} async-done(((f32[32,4,128]{2,1,0:T(4,128)}), f32[32,4,128]{2,1,0:T(4,128)S(1)}, u32[]{:S(2)}, u32[]{:S(2)}) %all-to-all-start) | async-done | bytes 65568 | tf_op jit(solution)/shard_map/weight_plane/all_to_all | solution.py:312
  27.3 41.0 %all_to_all.15.got = bf16[32,24,128]{2,1,0:T(8,128)(2,1)S(1)} all-to-all(bf16[32,24,128]{2,1,0:T(8,128)(2,1)S(1)} %join.1), channel_id=1, replica_groups={{576,608,640,672,704,736,768,800,832,864,896,928,960,992,0,32,64,96,128..., dimensions={0} | all-to-all | bytes 393216 | tf_op jit(solution)/shard_map/along_z/all_to_all | solution.py:334
  68.2 0.7 regroup.1
  69.0 0.0 copy-start
  69.0 10.8 %all_to_all.16 = bf16[16,112,128]{2,1,0:T(8,128)(2,1)S(1)} all-to-all(bf16[16,112,128]{2,1,0:T(8,128)(2,1)S(1)} %regroup.1), channel_id=1, replica_groups={{20,22,16,18,28,30,24,26,4,6,0,2,12,14,8,10},{21,23,17,19,29,31,25,27,5..., dimensions={0} | all-to-all | bytes 917504 | tf_op jit(solution)/shard_map/in_plane/all_to_all | solution.py:342
  79.8 0.0 copy-start.3
  79.8 5.3 %all-gather = bf16[32,112,128]{2,1,0:T(8,128)(2,1)S(1)} all-gather(bf16[16,112,128]{2,1,0:T(8,128)(2,1)S(1)} %all_to_all.16), channel_id=2, replica_groups=mesh['z'=32,'x'=4,'col'=4,'rep'=2] {'rep'}, dimensions={0}, use_global_device_ids=true | all-gather | bytes 1376256 | tf_op jit(solution)/shard_map/on_chip/all_gather | solution.py:346
  85.1 0.0 copy-done
  85.1 0.0 copy-done.3
  85.1 0.0 copy-done.4
  85.1 5.0 %update.1 = (f32[64,4096]{1,0:T(8,128)}, f32[1,4096]{1,0:T(1,128)}, f32[64,256]{1,0:T(8,128)}, f32[64,256]{1,0:T(8,128)}) custom-call(bf16[2,16,112,128]{3,2,1,0:T(8,128)(2,1)S(1)} %bitcast.9, f32[64,4096]{1,0:T(8,128)S(1)} %bitcast.10, f32[1,4096]{1,0:T(1,128)S(1)} %bitcast.11, f32[64,256]{1,0:T(8,128)S(1)} %copy-done.1, f32[64,256]{1,0:T(8,128)S(1)} %copy-done.3), custom_call_target="tpu_custom_call" | custom-call | tf_op jit(solution)/shard_map/update/pallas_call | solution.py:262
  (2 shorter events, 0.1 us)
Async XLA Ops:
  0.6 22.4 %copy-start.7 = (f32[128,4]{0,1:T(4,128)S(1)}, f32[128,4]{0,1:T(4,128)}, u32[]{:S(2)}) copy-start(f32[128,4]{0,1:T(4,128)} %param.13) | copy-start | bytes 6148
  2.3 20.8 %copy-start.1 = (f32[64,256]{1,0:T(8,128)S(1)}, f32[64,256]{1,0:T(8,128)}, u32[]{:S(2)}) copy-start(f32[64,256]{1,0:T(8,128)} %projection.3) | copy-start | bytes 196612
  2.3 20.8 %copy-start.2 = (bf16[128,256]{1,0:T(8,128)(2,1)S(1)}, bf16[128,256]{1,0:T(8,128)(2,1)}, u32[]{:S(2)}) copy-start(bf16[128,256]{1,0:T(8,128)(2,1)} %output_grad.3) | copy-start | bytes 196612
  2.3 24.9 %all-to-all-start = ((f32[32,4,128]{2,1,0:T(4,128)}), f32[32,4,128]{2,1,0:T(4,128)S(1)}, u32[]{:S(2)}, u32[]{:S(2)}) async-start(f32[32,4,128]{2,1,0:T(4,128)} %weight.1), calls=%async_computation | async-start | bytes 131072 | tf_op jit(solution)/shard_map/weight_plane/all_to_all | solution.py:312
  23.0 0.7 copy-start.6
  23.0 0.7 copy-start.5
  69.0 16.1 %copy-start = (f32[4096,64]{0,1:T(8,128)S(1)}, f32[4096,64]{0,1:T(8,128)}, u32[]{:S(2)}) copy-start(f32[4096,64]{0,1:T(8,128)} %param.14) | copy-start | bytes 3145732
  79.8 5.3 %copy-start.3 = (f32[64,256]{1,0:T(8,128)S(1)}, f32[64,256]{1,0:T(8,128)}, u32[]{:S(2)}) copy-start(f32[64,256]{1,0:T(8,128)} %projection_state.1) | copy-start | bytes 196612
  79.8 5.3 %copy-start.4 = (f32[4096]{0:T(1024)S(1)}, f32[4096]{0:T(1024)}, u32[]{:S(2)}) copy-start(f32[4096]{0:T(1024)} %param.15) | copy-start | bytes 49156

commit v5 on v4

--- a/solution.py
+++ b/solution.py
@@ -12,7 +12,7 @@
 epsilon = 1e-06
 
 X = 4
-Z_FIRST = 18
+Z_FIRST = 20
 SHARE_FIRST = (3, 3)
 ROWS_FIRST = (2, 2)
 CAP = 6

time: 90.4 us -> 89.8 us (level)
    all_to_all x1, blocking collectives: 41 us -> 39.6 us  [shards(): got = lax.all_to_all(sent, 'z', 0, 0, axis_index_groups=ring, tiled=True)]
where the time goes in v5:
time: 89.8 us; the launch traced here: 89.4 us
  blocking collectives  56.4 us (63%)
  starting transfers between devices  20.7 us (23%)
  Pallas kernels  8.27 us (9%)
  waiting for transfers between devices  2.62 us (3%)
    all_to_all x1, blocking collectives, shards(): got = lax.all_to_all(sent, 'z', 0, 0, axis_index_groups=ring, tiled=True)  39.6 us
    all_to_all x1, starting transfers between devices, shards(): lax.all_to_all(shares, PLANE, 0, 0, axis_index_groups=share_group, tiled=...  20.7 us
    all_to_all x1, blocking collectives, shards(): lax.all_to_all(sent, ('x', 'col'), 0, 0, axis_index_groups=[rows_order],...  10.8 us
    pallas_call x5, Pallas kernels, call(): pl.pallas_call(kernel, out_shape=outs, in_specs=[pl.BlockSpec(memory_spac...  8.27 us
    all_gather x1, blocking collectives, shards(): got = lax.all_gather(got, 'rep')  5.99 us
    all_to_all x1, waiting for transfers between devices, shards(): lax.all_to_all(shares, PLANE, 0, 0, axis_index_groups=share_group, tiled=...  2.62 us
  transfers between devices with their start and end apart: 1, of which 1 were waited for; matrix products, arithmetic and copies ran while one was open for 0% of the time, Pallas kernels for 1%

profile of v5, /device:TPU:1, one launch (start us, length us, event | category | flops | bytes accessed | tf_op | source)
XLA Modules:
  0.0 89.4 jit_solution(17016728286383690033)
XLA Ops:
  0.6 0.0 copy-start.7
  0.6 1.6 %weight.1 = f32[32,4,128]{2,1,0:T(4,128)} custom-call(bf16[128,256]{1,0:T(8,128)(2,1)} %output_grad.3, bf16[64,128]{1,0:T(8,128)(2,1)} %bitcast.15), custom_call_target="tpu_custom_call" | custom-call | tf_op jit(solution)/shard_map/weight/pallas_call | solution.py:262
  2.3 0.0 copy-start.1
  2.3 0.0 copy-start.2
  2.3 20.7 %all-to-all-start = ((f32[32,4,128]{2,1,0:T(4,128)}), f32[32,4,128]{2,1,0:T(4,128)S(1)}, u32[]{:S(2)}, u32[]{:S(2)}) async-start(f32[32,4,128]{2,1,0:T(4,128)} %weight.1), calls=%async_computation | async-start | bytes 131072 | tf_op jit(solution)/shard_map/weight_plane/all_to_all | solution.py:312
  23.0 0.0 copy-start.6
  23.0 0.0 copy-start.5
  23.1 0.0 copy-done.7
  23.1 0.0 copy-done.1
  23.1 0.0 copy-done.2
  23.1 0.6 copy-done.6
  23.7 0.0 copy-done.5
  23.7 0.9 route.1.sent
  24.6 2.6 %all-to-all-done.shares = f32[32,4,128]{2,1,0:T(4,128)S(1)} async-done(((f32[32,4,128]{2,1,0:T(4,128)}), f32[32,4,128]{2,1,0:T(4,128)S(1)}, u32[]{:S(2)}, u32[]{:S(2)}) %all-to-all-start) | async-done | bytes 65568 | tf_op jit(solution)/shard_map/weight_plane/all_to_all | solution.py:312
  27.3 39.6 %all_to_all.15.got = bf16[32,24,128]{2,1,0:T(8,128)(2,1)S(1)} all-to-all(bf16[32,24,128]{2,1,0:T(8,128)(2,1)S(1)} %join.1), channel_id=1, replica_groups={{640,672,704,736,768,800,832,864,896,928,960,992,0,32,64,96,128,160,192..., dimensions={0} | all-to-all | bytes 393216 | tf_op jit(solution)/shard_map/along_z/all_to_all | solution.py:334
  66.9 0.7 regroup.1
  67.6 0.0 copy-start
  67.7 10.8 %all_to_all.16 = bf16[16,112,128]{2,1,0:T(8,128)(2,1)S(1)} all-to-all(bf16[16,112,128]{2,1,0:T(8,128)(2,1)S(1)} %regroup.1), channel_id=1, replica_groups={{20,22,16,18,28,30,24,26,4,6,0,2,12,14,8,10},{21,23,17,19,29,31,25,27,5..., dimensions={0} | all-to-all | bytes 917504 | tf_op jit(solution)/shard_map/in_plane/all_to_all | solution.py:342
  78.4 0.0 copy-start.3
  78.5 6.0 %all-gather = bf16[32,112,128]{2,1,0:T(8,128)(2,1)S(1)} all-gather(bf16[16,112,128]{2,1,0:T(8,128)(2,1)S(1)} %all_to_all.16), channel_id=2, replica_groups=mesh['z'=32,'x'=4,'col'=4,'rep'=2] {'rep'}, dimensions={0}, use_global_device_ids=true | all-gather | bytes 1376256 | tf_op jit(solution)/shard_map/on_chip/all_gather | solution.py:346
  84.4 0.0 copy-done
  84.4 0.0 copy-done.3
  84.4 0.0 copy-done.4
  84.4 5.0 %update.1 = (f32[64,4096]{1,0:T(8,128)}, f32[1,4096]{1,0:T(1,128)}, f32[64,256]{1,0:T(8,128)}, f32[64,256]{1,0:T(8,128)}) custom-call(bf16[2,16,112,128]{3,2,1,0:T(8,128)(2,1)S(1)} %bitcast.9, f32[64,4096]{1,0:T(8,128)S(1)} %bitcast.10, f32[1,4096]{1,0:T(1,128)S(1)} %bitcast.11, f32[64,256]{1,0:T(8,128)S(1)} %copy-done.1, f32[64,256]{1,0:T(8,128)S(1)} %copy-done.3), custom_call_target="tpu_custom_call" | custom-call | tf_op jit(solution)/shard_map/update/pallas_call | solution.py:262
  (2 shorter events, 0.1 us)
Async XLA Ops:
  0.6 22.4 %copy-start.7 = (f32[128,4]{0,1:T(4,128)S(1)}, f32[128,4]{0,1:T(4,128)}, u32[]{:S(2)}) copy-start(f32[128,4]{0,1:T(4,128)} %param.13) | copy-start | bytes 6148
  2.3 20.8 %copy-start.1 = (f32[64,256]{1,0:T(8,128)S(1)}, f32[64,256]{1,0:T(8,128)}, u32[]{:S(2)}) copy-start(f32[64,256]{1,0:T(8,128)} %projection.3) | copy-start | bytes 196612
  2.3 20.8 %copy-start.2 = (bf16[128,256]{1,0:T(8,128)(2,1)S(1)}, bf16[128,256]{1,0:T(8,128)(2,1)}, u32[]{:S(2)}) copy-start(bf16[128,256]{1,0:T(8,128)(2,1)} %output_grad.3) | copy-start | bytes 196612
  2.3 24.9 %all-to-all-start = ((f32[32,4,128]{2,1,0:T(4,128)}), f32[32,4,128]{2,1,0:T(4,128)S(1)}, u32[]{:S(2)}, u32[]{:S(2)}) async-start(f32[32,4,128]{2,1,0:T(4,128)} %weight.1), calls=%async_computation | async-start | bytes 131072 | tf_op jit(solution)/shard_map/weight_plane/all_to_all | solution.py:312
  23.0 0.7 copy-start.6
  23.0 0.7 copy-start.5
  67.6 16.8 %copy-start = (f32[4096,64]{0,1:T(8,128)S(1)}, f32[4096,64]{0,1:T(8,128)}, u32[]{:S(2)}) copy-start(f32[4096,64]{0,1:T(8,128)} %param.14) | copy-start | bytes 3145732
  78.4 6.0 %copy-start.3 = (f32[64,256]{1,0:T(8,128)S(1)}, f32[64,256]{1,0:T(8,128)}, u32[]{:S(2)}) copy-start(f32[64,256]{1,0:T(8,128)} %projection_state.1) | copy-start | bytes 196612
  78.4 6.0 %copy-start.4 = (f32[4096]{0:T(1024)S(1)}, f32[4096]{0:T(1024)}, u32[]{:S(2)}) copy-start(f32[4096]{0:T(1024)} %param.15) | copy-start | bytes 49156
